TPU v7x, 512 devices: a whole 4x8x8 slice. The times are simulated.
512 devices in a mesh: row: 32 (over x_hi, y, core), col: 16 (over x_lo, z).
Axes of the slice: x: 4 (x_hi: 2, x_lo: 2; x = x_hi * 2 + x_lo), y: 8, z: 8, core: 2. Of those that a mesh axis runs over, the one named last changes fastest.
Arguments:
- prior: bfloat16 [65536, 256], P(('row', 'col')), may hold values from 0.1 to 2
- inv_degree: float32 [65536], P(('row', 'col')), may hold values from 0.03125 to 0.125
- seed_rows: int32 [8192], P(('row', 'col')), may hold values from 0 to 127, as said below
- seed_scores: bfloat16 [8192, 256], P(('row', 'col')), may hold values from 0.1 to 2
- block_mask: int32 [36864, 128, 128], P(('row', 'col')), may hold values 0 or 1
- block_row: int32 [36864], P(('row', 'col')), may hold values from 0 to 31, as said below
- block_col: int32 [36864], P(('row', 'col')), may hold values from 0 to 15, as said below
- block_live: int32 [512], P(('row', 'col')), may hold values from 9 to 72, as said below
Outputs:
- labels: bfloat16 [65536, 256], P(('row', 'col'))
Inputs may be any that keep to these rules, and one draw needn't show every extreme that they name: `seed_rows`: within one device's 16 entries the indices are distinct. Within one device's 72 slots, the pairs (block_row, block_col) are distinct. `block_col`: see block_row. `block_live`: some device uses all 72 slots.
All inputs are finite; a program needn't handle non-finite values. No bound on the sum of `block_mask` on one device may be relied on, other than what follows from the above.
Results may differ from a plain program's by a relative error of at most 0.015.
Values may be sent and summed in bfloat16 or wider, within the bound.
A program may use at most 64 MiB of HBM per device.

v0:
```python
import jax
import jax.numpy as jnp
from jax import lax
from jax.sharding import PartitionSpec as P

ITERS = 2


MIX_RATE = 0.9


def local(prior, inv_degree, seed_rows, seed_scores, block_mask, block_row, block_col, block_live):
    docs_dev, width = prior.shape
    slots, side = (block_mask.shape[0], block_mask.shape[1])
    target_blocks = lax.axis_size("row") * docs_dev // side
    live = block_live[0]
    slot_ids = jnp.arange(slots, dtype=jnp.int32)
    weights = (block_mask * (slot_ids < live).astype(jnp.int32)[:, None, None]).astype(jnp.bfloat16)
    hits = (seed_rows[:, None] == jnp.arange(docs_dev, dtype=jnp.int32)[None, :]).astype(
        jnp.bfloat16
    )
    seeded = jnp.dot(hits.T, seed_scores, preferred_element_type=jnp.float32)
    covered = jnp.sum(hits.astype(jnp.float32), axis=0) > 0.5
    base = (1.0 - MIX_RATE) * prior.astype(jnp.float32)
    factor = MIX_RATE * inv_degree[:, None]
    labels = prior
    for step in range(ITERS):
        sources = lax.all_gather(labels, "col", axis=0, tiled=True)
        src_blocks = sources.reshape(-1, side, width)
        picked = jnp.take(src_blocks, block_col, axis=0)
        products = jnp.einsum("sij,sjl->sil", weights, picked, preferred_element_type=jnp.float32)
        summed = jnp.zeros((target_blocks, side, width), jnp.float32).at[block_row].add(products)
        summed = summed.reshape(target_blocks * side, width)
        sums = lax.psum_scatter(
            summed.astype(jnp.bfloat16), "row", scatter_dimension=0, tiled=True
        ).astype(jnp.float32)
        fresh = factor * sums + base
        labels = jnp.where(covered[:, None], seeded, fresh).astype(jnp.bfloat16)
    return labels


def solution(mesh):
    return jax.shard_map(
        local,
        mesh=mesh,
        in_specs=(
            P(("row", "col"), None),
            P(("row", "col")),
            P(("row", "col")),
            P(("row", "col"), None),
            P(("row", "col"), None, None),
            P(("row", "col")),
            P(("row", "col")),
            P(("row", "col")),
        ),
        out_specs=P(("row", "col"), None),
        check_vma=False,
    )
```

profile of v0, /device:TPU:1, one launch (start us, length us, event | category | flops | bytes accessed | tf_op | source)
XLA Modules:
  0.0 504.6 jit_solution(6479234486084292138)
XLA Ops:
  6.5 0.0 copy-start
  6.5 0.0 all-gather.3.cloned.1.call-start
  6.5 0.7 all-gather.3.cloned.1.call-update
  7.3 0.0 reduce-scatter.3.cloned.1.call-start
  8.0 0.7 compare_select_fusion
  8.6 0.7 compare_select_fusion.1
  9.3 0.7 compare_and_fusion
  9.9 67.4 %all-gather.3.cloned.1.call-done = bf16[2048,256]{1,0:T(8,128)(2,1)} async-done(((bf16[128,256]{1,0:T(8,128)(2,1)}), bf16[2048,256]{1,0:T(8,128)(2,1)}) %all-gather.3.cloned.1.call-update) | async-done | bytes 1048592 | tf_op jit(solution)/shard_map/all_gather | solution.py:28
  77.4 6.8 %gather_fusion = bf16[72,128,256]{2,1,0:T(8,128)(2,1)} fusion(bf16[16,128,256]{2,1,0:T(8,128)(2,1)} %bitcast.7, s32[1024]{0:T(1024)S(1)} %pad_clamp_fusion), kind=kCustom, calls=%fused_computation.clone | custom fusion | bytes 9437472 | tf_op jit(solution)/shard_map/jit(_take)/gather | solution.py:30
  84.2 8.9 %fusion.2 = f32[72,128,256]{2,1,0:T(8,128)} fusion(bf16[72,128,256]{2,1,0:T(8,128)(2,1)} %gather_fusion, pred[72]{0:T(512)(128)(4,1)S(1)} %get-tuple-element.8, s32[72,128,128]{2,1,0:T(8,128)} %param.14, s32[72]{0:T(128)S(1)} %get-tuple-element.9), kind=kOutput, calls=%fused_computation.6 | convolution fusion | flops 608698368 | bytes 18874728 | tf_op jit(solution)/shard_map/sij,sjl->sil/dot_general | solution.py:31
  93.1 2.6 broadcast.23.clone
  95.6 23.4 %scatter_fusion = f32[32,128,256]{2,1,0:T(8,128)} fusion(f32[32,128,256]{2,1,0:T(8,128)} %broadcast.23.clone, s32[72]{0:T(128)S(1)} %compare_select_fusion.1, f32[72,128,256]{2,1,0:T(8,128)} %fusion.2), kind=kCustom, calls=%fused_computation.2 | custom fusion | flops 2359296 | bytes 28311840 | tf_op jit(solution)/shard_map/scatter-add | solution.py:32
  119.0 0.0 copy-start.3
  119.0 0.0 copy-start.2
  119.0 0.0 copy-start.1
  119.0 3.8 convert_element_type.47
  122.9 0.0 reduce-scatter.3.cloned.1.call-update
  122.9 0.0 all-gather.5.cloned.1.call-start
  123.0 0.0 copy-done.3
  123.0 0.1 convert_reduce_fusion
  123.1 0.0 copy-done.2
  123.1 129.7 %reduce-scatter.3.cloned.1.call-done = bf16[128,256]{1,0:T(8,128)(2,1)} async-done(((bf16[4096,256]{1,0:T(8,128)(2,1)}), bf16[128,256]{1,0:T(8,128)(2,1)}) %reduce-scatter.3.cloned.1.call-update) | async-done | bytes 65552 | tf_op jit(solution)/shard_map/reduce_scatter | solution.py:34
  252.8 0.0 copy-done
  252.8 0.0 copy-done.1
  252.8 1.8 select_convert_fusion.1
  254.6 0.0 all-gather.5.cloned.1.call-update
  254.6 0.0 reduce-scatter.5.cloned.1.call-start
  254.7 66.4 %all-gather.5.cloned.1.call-done = bf16[2048,256]{1,0:T(8,128)(2,1)} async-done(((bf16[128,256]{1,0:T(8,128)(2,1)}), bf16[2048,256]{1,0:T(8,128)(2,1)}) %all-gather.5.cloned.1.call-update) | async-done | bytes 1048592 | tf_op jit(solution)/shard_map/all_gather | solution.py:28
  321.1 6.8 %gather_fusion.1 = bf16[72,128,256]{2,1,0:T(8,128)(2,1)} fusion(bf16[16,128,256]{2,1,0:T(8,128)(2,1)} %bitcast.8, s32[1024]{0:T(1024)S(1)} %pad_clamp_fusion), kind=kCustom, calls=%fused_computation.1.clone | custom fusion | bytes 9437472 | tf_op jit(solution)/shard_map/jit(_take)/gather | solution.py:30
  327.9 8.9 %fusion = f32[72,128,256]{2,1,0:T(8,128)} fusion(bf16[72,128,256]{2,1,0:T(8,128)(2,1)} %gather_fusion.1, pred[72]{0:T(512)(128)(4,1)S(1)} %get-tuple-element.8, s32[72,128,128]{2,1,0:T(8,128)} %param.14, s32[72]{0:T(128)S(1)} %get-tuple-element.9), kind=kOutput, calls=%fused_computation.4 | convolution fusion | flops 608698368 | bytes 18874728 | tf_op jit(solution)/shard_map/sij,sjl->sil/dot_general | solution.py:31
  336.8 2.6 broadcast.23
  339.3 23.4 %scatter_fusion.1 = f32[32,128,256]{2,1,0:T(8,128)} fusion(f32[32,128,256]{2,1,0:T(8,128)} %broadcast.23, s32[72]{0:T(128)S(1)} %compare_select_fusion.1, f32[72,128,256]{2,1,0:T(8,128)} %fusion), kind=kCustom, calls=%fused_computation.3 | custom fusion | flops 2359296 | bytes 28311840 | tf_op jit(solution)/shard_map/scatter-add | solution.py:32
  362.8 3.8 convert_element_type.52
  366.6 0.0 reduce-scatter.5.cloned.1.call-update
  366.6 129.9 %reduce-scatter.5.cloned.1.call-done = bf16[128,256]{1,0:T(8,128)(2,1)} async-done(((bf16[4096,256]{1,0:T(8,128)(2,1)}), bf16[128,256]{1,0:T(8,128)(2,1)}) %reduce-scatter.5.cloned.1.call-update) | async-done | bytes 65552 | tf_op jit(solution)/shard_map/reduce_scatter | solution.py:34
  496.5 1.6 select_convert_fusion
  (3 shorter events, 0.0 us)
Async XLA Ops:
  6.5 246.3 %copy-start = (bf16[16,256]{1,0:T(8,128)(2,1)S(1)}, bf16[16,256]{1,0:T(8,128)(2,1)}, u32[]{:S(2)}) copy-start(bf16[16,256]{1,0:T(8,128)(2,1)} %param.13) | copy-start | bytes 24580
  6.5 70.8 %all-gather.3.cloned.1.call-start = ((), (), s32[]{:S(2)}) async-start(), calls=%async_computation.2 | async-start | bytes 1114112 | tf_op jit(solution)/shard_map/all_gather | solution.py:28
  7.3 245.6 %reduce-scatter.3.cloned.1.call-start = ((), (), s32[]{:S(2)}) async-start(), calls=%async_computation.3 | async-start | bytes 2162688 | tf_op jit(solution)/shard_map/reduce_scatter | solution.py:34
  119.0 3.9 copy-start.3
  119.0 4.0 copy-start.2
  119.0 133.8 %copy-start.1 = (bf16[128,256]{1,0:T(8,128)(2,1)S(1)}, bf16[128,256]{1,0:T(8,128)(2,1)}, u32[]{:S(2)}) copy-start(bf16[128,256]{1,0:T(8,128)(2,1)} %param.10) | copy-start | bytes 196612
  122.9 198.2 %all-gather.5.cloned.1.call-start = ((), (), s32[]{:S(2)}) async-start(), calls=%async_computation.4 | async-start | bytes 1114112 | tf_op jit(solution)/shard_map/all_gather | solution.py:28
  254.6 241.9 %reduce-scatter.5.cloned.1.call-start = ((), (), s32[]{:S(2)}) async-start(), calls=%async_computation.5 | async-start | bytes 2162688 | tf_op jit(solution)/shard_map/reduce_scatter | solution.py:34
Sparse Core Ops, SparseCore 0:
  9.4 67.8 all-gather.2
  123.0 129.7 reduce-scatter.2
  255.1 65.9 all-gather.4
  366.7 129.6 reduce-scatter.4
where the time goes:
time: 509 us; the launch traced here: 505 us
  waiting for transfers between devices  394 us (77%)
  other arithmetic  58.2 us (11%)
  matrix products  19.5 us (4%)
  local copies, waits for them, and re-layouts  18.8 us (4%)
  between operations  13.8 us (3%)
    reduce_scatter x2, waiting for transfers between devices, local(): lax.psum_scatter(summed.astype(jnp.bfloat16), 'row', scatter_dimension=0,...  260 us
    all_gather x2, waiting for transfers between devices, local(): sources = lax.all_gather(labels, 'col', axis=0, tiled=True)  134 us
    scatter-add x2, other arithmetic, local(): jnp.zeros((target_blocks, side, width), jnp.float32).at[block_row]  46.8 us
    dot_general x2, matrix products, local(): jnp.einsum('sij,sjl->sil', weights, picked, preferred_element_type=jnp.fl...  17.7 us
    gather x2, local copies, waits for them, and re-layouts, local(): picked = jnp.take(src_blocks, block_col, axis=0)  13.6 us
  transfers between devices with their start and end apart: 4, of which 4 were waited for; matrix products, arithmetic and copies ran while one was open for 0% of the time, Pallas kernels for 0%

commit v1 on v0

v1 whole, which is shorter than its diff:
```python
import functools

import jax
import jax.numpy as jnp
from jax import lax
from jax.experimental import pallas as pl
from jax.experimental.pallas import tpu as pltpu
from jax.sharding import PartitionSpec as P

ITERS = 2
MIX_RATE = 0.9
BLK = 128
HALF = 128
HALVES = 2
NZ, NY = 8, 8
LEAD = 0

ROUNDS = (
    (("P", (0, 0), (0, -1)), ("N", (0, 0), (0, 1)), ("X", (0, 0), (1, 0))),
    (("P", (0, -1), (0, -2)), ("N", (0, 1), (0, 2)), ("X", (0, 1), (1, 1))),
    (("P", (0, -2), (0, -3)), ("N", (0, 2), (0, 3)), ("X", (0, 2), (1, 2))),
    (("P", (0, -3), (0, -4)), ("N", (1, 2), (1, 3)), ("X", (0, -2), (1, -2))),
    (("P", (1, -2), (1, -3)), ("N", (1, 3), (1, 4)), ("X", (0, -1), (1, -1))),
)
ORDER = (4, 3, -3, 2, -2, 1, -1, 0)
MCHUNKS = 4


def slot(pos):
    return (pos[0] * NZ + pos[1] % NZ) * BLK


def at(j):
    return ORDER.index(j) * 2 * BLK


def kernel(
    prior_ref, inv_ref, seed_rows_ref, seed_scores_ref, mask_hbm, brow_ref, bcol_ref, live_ref,
    out_ref,
    mask_v, wblk, weights, src, csend, crecv, own, ysend, yrecv, xsend, xrecv,
    base, factor, covered, table_v, table_s, send_sem, recv_sem, local_sem,
):
    row, col = lax.axis_index("row"), lax.axis_index("col")
    core = row % 2
    y = (row // 2) % NY
    xh = row // (2 * NY)
    z = col % NZ
    xl = col // NZ
    slots = mask_v.shape[0]

    def rowof(a, b, c):
        return (a * NY + b) * 2 + c

    peers = {
        "P": (row, xl * NZ + (z + 1) % NZ),
        "N": (row, xl * NZ + (z + NZ - 1) % NZ),
        "X": (row, (1 - xl) * NZ + z),
        "C": (rowof(xh, y, 1 - core), col),
        "U": (rowof(xh, (y + 1) % NY, core), col),
        "D": (rowof(xh, (y + NY - 1) % NY, core), col),
        "H": (rowof(1 - xh, y, core), col),
    }

    mask_copy = pltpu.make_async_copy(mask_hbm, mask_v, local_sem.at[0])
    mask_copy.start()

    barrier = pltpu.get_barrier_semaphore()
    for peer in peers.values():
        pl.semaphore_signal(barrier, inc=1, device_id=peer, device_id_type=pl.DeviceIdType.MESH)

    for h in range(HALVES):
        src[0, h, 0:BLK, :] = prior_ref[:, h * HALF : (h + 1) * HALF]

    pl.semaphore_wait(barrier, len(peers))

    started = []

    def send(source, target, peer):
        n = len(started)
        copy = pltpu.make_async_remote_copy(
            src_ref=source,
            dst_ref=target,
            send_sem=send_sem.at[n],
            recv_sem=recv_sem.at[n],
            device_id=peers[peer],
            device_id_type=pl.DeviceIdType.MESH,
        )
        copy.start()
        started.append(copy)
        return copy

    def prepare():
        spot = lax.broadcasted_iota(jnp.int32, (8, 128), 0) * 128 + lax.broadcasted_iota(
            jnp.int32, (8, 128), 1
        )
        live = live_ref[0]

        def mark(s, acc):
            key = brow_ref[s] * (2 * NZ) + bcol_ref[s]
            key = jnp.where(s < live, key, -1)
            return jnp.where(spot == key, s + 1, acc)

        table_v[...] = lax.fori_loop(0, slots, mark, jnp.zeros((8, 128), jnp.int32))
        table_copy = pltpu.make_async_copy(table_v, table_s, local_sem.at[1])
        table_copy.start()

        docs = lax.broadcasted_iota(jnp.int32, (BLK, seed_rows_ref.shape[1]), 0)
        hits = (docs == seed_rows_ref[...]).astype(jnp.float32)
        seeded = jnp.dot(
            hits.astype(jnp.bfloat16), seed_scores_ref[...], preferred_element_type=jnp.float32
        )
        cov = jnp.broadcast_to(jnp.sum(hits, axis=1, keepdims=True), (BLK, HALF))
        covered[...] = cov
        eye = lax.broadcasted_iota(jnp.int32, (BLK, BLK), 0) == lax.broadcasted_iota(
            jnp.int32, (BLK, BLK), 1
        )
        inv = jnp.sum(jnp.where(eye, inv_ref[...], 0.0), axis=1, keepdims=True)
        factor[...] = jnp.broadcast_to(MIX_RATE * inv, (BLK, HALF))
        for h in range(HALVES):
            cols = slice(h * HALF, (h + 1) * HALF)
            base[h] = jnp.where(
                cov > 0.5,
                seeded[:, cols],
                (1.0 - MIX_RATE) * prior_ref[:, cols].astype(jnp.float32),
            )
        mask_copy.wait()
        wblk[0] = jnp.zeros((BLK, BLK), jnp.bfloat16)

        @pl.loop(0, slots)
        def _(s):
            wblk[s + 1] = mask_v[s].astype(jnp.float32).astype(jnp.bfloat16)

        table_copy.wait()

    def build(first, last):
        @pl.loop(first, last)
        def _(rb):
            kk = rb // 16
            p = (rb // 2) % 8
            xx = rb % 2
            j = (4 - (p + 1) // 2) * (2 * (p % 2) - 1)
            b = rowof((xh + 1 + xx) % 2, (y + j + NY) % NY, (core + 1 + kk) % 2)
            for dx in range(2):
                for dz in range(NZ):
                    c = ((xl + dx) % 2) * NZ + (z + dz) % NZ
                    which = table_s[b // 8, (b % 8) * 16 + c]
                    weights[
                        pl.ds(pl.multiple_of(rb * BLK, BLK), BLK),
                        (dx * NZ + dz) * BLK : (dx * NZ + dz + 1) * BLK,
                    ] = wblk[which]

    def flow(it, h):
        arrived = {}
        for n, steps in enumerate(ROUNDS):
            for way, here, there in steps:
                if here in arrived:
                    arrived.pop(here).wait_recv()
                arrived[there] = send(
                    src.at[it, h, pl.ds(slot(here), BLK)],
                    src.at[it, h, pl.ds(slot(there), BLK)],
                    way,
                )
            if it == 0 and h == 0:
                if n == 0:
                    prepare()
                else:
                    build((n - 1) * 8, n * 8)
            yield
        for copy in arrived.values():
            copy.wait_recv()
        labels = src.at[it, h]
        rows = 2 * NY * BLK // MCHUNKS
        core_copies = []
        for m in range(MCHUNKS):
            part = jnp.dot(
                weights[m * rows : (m + 1) * rows, :],
                labels[...],
                preferred_element_type=jnp.float32,
            )
            csend[it, h, m * rows : (m + 1) * rows, :] = part.astype(jnp.bfloat16)
            where = pl.ds(m * rows, rows)
            core_copies.append(send(csend.at[it, h, where], crecv.at[it, h, where], "C"))
            yield
        for m in range(MCHUNKS):
            first = 2 * NY * BLK + m * rows
            own[h, m * rows : (m + 1) * rows, :] = jnp.dot(
                weights[first : first + rows, :],
                labels[...],
                preferred_element_type=jnp.float32,
            )
            yield

        waited = set()

        def local(j, xx, n=1):
            first = at(j) + xx * BLK
            m = first // rows
            if m not in waited:
                waited.add(m)
                core_copies[m].wait_recv()
            where = slice(first, first + n * BLK)
            return own[h, where, :] + crecv[it, h, where, :].astype(jnp.float32)

        up, down = ysend.at[it, h, 0], ysend.at[it, h, 1]
        rup, rdown = yrecv.at[it, h, 0], yrecv.at[it, h, 1]
        one, both = pl.ds(0, BLK), pl.ds(0, 2 * BLK)
        up[0, 0:BLK, :] = local(4, 0).astype(jnp.bfloat16)
        u = send(up.at[0, one], rup.at[0, one], "U")
        down[0, 0:BLK, :] = local(4, 1).astype(jnp.bfloat16)
        d = send(down.at[0, one], rdown.at[0, one], "D")
        yield
        for step in (1, 2, 3):
            j = 4 - step
            if step == 1:
                up[1, BLK:, :] = local(j, 1).astype(jnp.bfloat16)
                down[1, 0:BLK, :] = local(-j, 0).astype(jnp.bfloat16)
                u.wait_recv()
                up[1, 0:BLK, :] = (local(j, 0) + rup[0, 0:BLK, :].astype(jnp.float32)).astype(
                    jnp.bfloat16
                )
            else:
                u.wait_recv()
                up[step] = (local(j, 0, 2) + rup[step - 1].astype(jnp.float32)).astype(jnp.bfloat16)
            u = send(up.at[step, both], rup.at[step, both], "U")
            d.wait_recv()
            if step == 1:
                down[1, BLK:, :] = (local(-j, 1) + rdown[0, 0:BLK, :].astype(jnp.float32)).astype(
                    jnp.bfloat16
                )
            else:
                down[step] = (local(-j, 0, 2) + rdown[step - 1].astype(jnp.float32)).astype(
                    jnp.bfloat16
                )
            d = send(down.at[step, both], rdown.at[step, both], "D")
            yield
        u.wait_recv()
        d.wait_recv()
        pieces = [
            local(0, xx)
            + rup[3, xx * BLK : (xx + 1) * BLK, :].astype(jnp.float32)
            + rdown[3, xx * BLK : (xx + 1) * BLK, :].astype(jnp.float32)
            for xx in (0, 1)
        ]
        xsend[it, h] = pieces[0].astype(jnp.bfloat16)
        x = send(xsend.at[it, h], xrecv.at[it, h], "H")
        own[h, at(0) + BLK : at(0) + 2 * BLK, :] = pieces[1]
        yield
        x.wait_recv()
        total = own[h, at(0) + BLK : at(0) + 2 * BLK, :] + xrecv[it, h].astype(jnp.float32)
        mixed = jnp.where(covered[...] > 0.5, base[h], factor[...] * total + base[h])
        if it == ITERS - 1:
            out_ref[:, h * HALF : (h + 1) * HALF] = mixed.astype(jnp.bfloat16)
        else:
            src[it + 1, h, 0:BLK, :] = mixed.astype(jnp.bfloat16)

    def stream(h):
        for it in range(ITERS):
            yield from flow(it, h)

    streams = [stream(h) for h in range(HALVES)]
    done = object()
    for _ in range(LEAD):
        next(streams[0])
    while streams:
        streams = [s for s in streams if next(s, done) is not done]
    for copy in started:
        copy.wait_send()


COPIES = 28 * ITERS * HALVES


def local(prior, inv_degree, seed_rows, seed_scores, block_mask, block_row, block_col, block_live):
    slots = block_mask.shape[0]
    vmem = pl.BlockSpec(memory_space=pltpu.VMEM)
    smem = pl.BlockSpec(memory_space=pltpu.SMEM)
    bf16, f32 = jnp.bfloat16, jnp.float32
    targets, sources = 4 * NY * BLK, 2 * NZ * BLK
    return pl.pallas_call(
        kernel,
        out_shape=jax.ShapeDtypeStruct(prior.shape, bf16),
        in_specs=[vmem, vmem, vmem, vmem, pl.BlockSpec(memory_space=pl.ANY), smem, smem, smem],
        out_specs=vmem,
        scratch_shapes=[
            pltpu.VMEM((slots, BLK, BLK), jnp.int32),
            pltpu.VMEM((slots + 1, BLK, BLK), bf16),
            pltpu.VMEM((targets, sources), bf16),
            pltpu.VMEM((ITERS, HALVES, sources, HALF), bf16),
            pltpu.VMEM((ITERS, HALVES, targets // 2, HALF), bf16),
            pltpu.VMEM((ITERS, HALVES, targets // 2, HALF), bf16),
            pltpu.VMEM((HALVES, targets // 2, HALF), f32),
            pltpu.VMEM((ITERS, HALVES, 2, 4, 2 * BLK, HALF), bf16),
            pltpu.VMEM((ITERS, HALVES, 2, 4, 2 * BLK, HALF), bf16),
            pltpu.VMEM((ITERS, HALVES, BLK, HALF), bf16),
            pltpu.VMEM((ITERS, HALVES, BLK, HALF), bf16),
            pltpu.VMEM((HALVES, BLK, HALF), f32),
            pltpu.VMEM((BLK, HALF), f32),
            pltpu.VMEM((BLK, HALF), f32),
            pltpu.VMEM((8, 128), jnp.int32),
            pltpu.SMEM((8, 128), jnp.int32),
            pltpu.SemaphoreType.DMA((COPIES,)),
            pltpu.SemaphoreType.DMA((COPIES,)),
            pltpu.SemaphoreType.DMA((2,)),
        ],
        compiler_params=pltpu.CompilerParams(
            collective_id=0, has_side_effects=True, vmem_limit_bytes=56 * 1024 * 1024
        ),
        name="propagate",
    )(
        prior,
        inv_degree.reshape(1, -1),
        seed_rows.reshape(1, -1),
        seed_scores,
        block_mask,
        block_row,
        block_col,
        block_live,
    )


def solution(mesh):
    return jax.shard_map(
        local,
        mesh=mesh,
        in_specs=(
            P(("row", "col"), None),
            P(("row", "col")),
            P(("row", "col")),
            P(("row", "col"), None),
            P(("row", "col"), None, None),
            P(("row", "col")),
            P(("row", "col")),
            P(("row", "col")),
        ),
        out_specs=P(("row", "col"), None),
        check_vma=False,
    )
```

time: 509 us -> 119 us (0.23)
  the two profiles are of different devices: /device:TPU:1 before, /device:TPU:8 now
where the time goes in v1:
time: 119 us; the launch traced here: 118 us
  Pallas kernels  116 us (97%)
  local copies, waits for them, and re-layouts  1.47 us (1%)
    pallas_call x1, Pallas kernels, local(): pl.pallas_call(kernel, out_shape=jax.ShapeDtypeStruct(prior.shape, bf16),...  116 us

profile of v1, /device:TPU:8, one launch (start us, length us, event | category | flops | bytes accessed | tf_op | source)
XLA Modules:
  0.0 118.5 jit_solution(944367314353058355)
XLA Ops:
  0.7 116.3 %propagate.1 = bf16[128,256]{1,0:T(8,128)(2,1)} custom-call(bf16[128,256]{1,0:T(8,128)(2,1)} %prior_ref.1, f32[1,128]{1,0:T(1,128)} %bitcast.2, s32[1,16]{1,0:T(1,128)} %bitcast.3, bf16[16,256]{1,0:T(8,128)(2,1)} %seed_scores_ref.1, s32[72,128,128]{2,1,0:T(8,128)} %mask_hbm.1, s32[72]{0:T(128)} %brow_ref.1, s32[72]{0:T(128)} %bcol_ref.1, s32[1]{0:T(128)S(6)} %copy.10.live_ref), custom_call_target="tpu_custom_call" | custom-call | tf_op jit(solution)/shard_map/propagate/pallas_call | solution.py:279
  117.0 1.5 %copy.11 = bf16[128,256]{1,0:T(8,128)(2,1)} copy(bf16[128,256]{1,0:T(8,128)(2,1)} %propagate.1) | data formatting | bytes 131072

commit v2 on v0

v2 whole, which is shorter than its diff:
```python
import jax
import jax.numpy as jnp
from jax import lax
from jax.experimental import pallas as pl
from jax.experimental.pallas import tpu as pltpu
from jax.sharding import PartitionSpec as P

ITERS = 2
MIX_RATE = 0.9
BLK = 128
NZ, NY = 8, 8

GROUPS = (
    ((0, 0), (0, 2), (0, 6), (1, 0), (0, 1), (0, 7)),
    ((0, 3), (0, 5), (1, 2), (1, 6), (1, 1), (1, 7)),
    ((0, 4), (1, 3), (1, 5), (1, 4)),
)
SLOTS = sum(GROUPS, ())
ORDER = (4, 3, -3, 2, -2, 1, -1, 0)
PIECES = len(ORDER) * BLK
ROWS = 512


def slot(dx, dz):
    return SLOTS.index((dx, dz % NZ)) * BLK


def kernel(
    prior_ref, inv_ref, seed_rows_ref, seed_scores_ref, mask_hbm, brow_ref, bcol_ref, live_ref,
    out_ref,
    mask_v, wblk, weights, src, csend, crecv, acc, ysend, yrecv, xsend, xrecv, mine,
    base, factor, covered, table_v, table_s, send_sem, recv_sem, local_sem,
):
    f32, bf16 = jnp.float32, jnp.bfloat16
    width = prior_ref.shape[1]
    row, col = lax.axis_index("row"), lax.axis_index("col")
    core = row % 2
    y = (row // 2) % NY
    xh = row // (2 * NY)
    z = col % NZ
    xl = col // NZ
    slots = mask_v.shape[0]

    def rowof(a, b, c):
        return (a * NY + b) * 2 + c

    def along_z(d):
        return (row, xl * NZ + (z + d + NZ) % NZ)

    def along_y(d):
        return (rowof(xh, (y + d + NY) % NY, core), col)

    peers = {
        "X": (row, (1 - xl) * NZ + z),
        "C": (rowof(xh, y, 1 - core), col),
        "H": (rowof(1 - xh, y, core), col),
    }
    for d in (1, 2, -1, -2):
        peers["z", d] = along_z(d)
        peers["y", d] = along_y(d)

    mask_copy = pltpu.make_async_copy(mask_hbm, mask_v, local_sem.at[0])
    mask_copy.start()

    barrier = pltpu.get_barrier_semaphore()
    for peer in peers.values():
        pl.semaphore_signal(barrier, inc=1, device_id=peer, device_id_type=pl.DeviceIdType.MESH)

    src[0, slot(0, 0) : slot(0, 0) + BLK, :] = prior_ref[...]

    started = []

    def send(source, target, peer):
        n = len(started)
        copy = pltpu.make_async_remote_copy(
            src_ref=source,
            dst_ref=target,
            send_sem=send_sem.at[n],
            recv_sem=recv_sem.at[n],
            device_id=peers[peer],
            device_id_type=pl.DeviceIdType.MESH,
        )
        copy.start()
        started.append(copy)
        return copy

    def prepare_table():
        spot = lax.broadcasted_iota(jnp.int32, (8, 128), 0) * 128 + lax.broadcasted_iota(
            jnp.int32, (8, 128), 1
        )
        live = live_ref[0]

        def mark(s, table):
            key = brow_ref[s] * (2 * NZ) + bcol_ref[s]
            key = jnp.where(s < live, key, -1)
            return jnp.where(spot == key, s + 1, table)

        table_v[...] = lax.fori_loop(0, slots, mark, jnp.zeros((8, 128), jnp.int32))
        copy = pltpu.make_async_copy(table_v, table_s, local_sem.at[1])
        copy.start()
        return copy

    def prepare_labels():
        docs = lax.broadcasted_iota(jnp.int32, (BLK, seed_rows_ref.shape[1]), 0)
        hits = (docs == seed_rows_ref[...]).astype(f32)
        seeded = jnp.dot(hits.astype(bf16), seed_scores_ref[...], preferred_element_type=f32)
        cov = jnp.broadcast_to(jnp.sum(hits, axis=1, keepdims=True), (BLK, width))
        covered[...] = cov
        eye = lax.broadcasted_iota(jnp.int32, (BLK, BLK), 0) == lax.broadcasted_iota(
            jnp.int32, (BLK, BLK), 1
        )
        inv = jnp.sum(jnp.where(eye, inv_ref[...], 0.0), axis=1, keepdims=True)
        factor[...] = jnp.broadcast_to(MIX_RATE * inv, (BLK, width))
        base[...] = jnp.where(cov > 0.5, seeded, (1.0 - MIX_RATE) * prior_ref[...].astype(f32))

    def convert():
        mask_copy.wait()
        wblk[0] = jnp.zeros((BLK, BLK), bf16)

        @pl.loop(0, slots)
        def _(s):
            wblk[s + 1] = mask_v[s].astype(f32).astype(bf16)

    def build(group):
        @pl.loop(0, 4)
        def _(q):
            kk = q // 2
            xx = q % 2
            for p, j in enumerate(ORDER):
                b = rowof((xh + 1 + xx) % 2, (y + j + NY) % NY, (core + 1 + kk) % 2)
                first = pl.multiple_of(q * PIECES + p * BLK, BLK)
                for dx, dz in group:
                    c = ((xl + dx) % 2) * NZ + (z + dz) % NZ
                    which = table_s[b // 8, (b % 8) * 16 + c]
                    weights[pl.ds(first, BLK), slot(dx, dz) : slot(dx, dz) + BLK] = wblk[which]

    def product(it, n, first):
        k = slot(*GROUPS[n][0])
        depth = len(GROUPS[n]) * BLK
        return jnp.dot(
            weights[first : first + ROWS, k : k + depth],
            src[it, k : k + depth, :],
            preferred_element_type=f32,
        )

    def products(it, n):
        for first in range(0, 4 * PIECES, ROWS):
            part = product(it, n, first)
            if n:
                part = part + acc[first : first + ROWS, :]
            acc[first : first + ROWS, :] = part

    half = BLK // 2
    table_copy = prepare_table()
    prepare_labels()
    pl.semaphore_wait(barrier, len(peers))

    for it in range(ITERS):
        coming = {}

        def block(pos, part):
            return src.at[it, pl.ds(slot(*pos) + part * half, half)]

        def take(dx, dz, part):
            copy = coming.pop((dx, dz % NZ, part), None)
            if copy is not None:
                copy.wait_recv()

        def pass_on(dx, dz, part, way, there):
            take(dx, dz, part)
            coming[there[0], there[1] % NZ, part] = send(
                block((dx, dz), part), block(there, part), way
            )

        for part in (0, 1):
            pass_on(0, 0, part, ("z", 2), (0, -2))
            pass_on(0, 0, part, ("z", -2), (0, 2))
            pass_on(0, 0, part, "X", (1, 0))
        for part in (0, 1):
            pass_on(0, 0, part, ("z", 1), (0, -1))
            pass_on(0, 0, part, ("z", -1), (0, 1))
        if it == 0:
            convert()
        for part in (0, 1):
            for d in (-2, 2):
                s = -1 if d > 0 else 1
                pass_on(0, d, part, "X", (1, d))
                pass_on(0, d, part, ("z", s), (0, d - s))
                if (part == 0) == (d < 0):
                    pass_on(0, d, part, ("z", 2 * s), (0, 4))
        for part in (0, 1):
            for d in (-1, 1):
                pass_on(0, d, part, "X", (1, d))
        if it == 0:
            table_copy.wait()
            build(GROUPS[0] + GROUPS[1])
        else:
            for part in (0, 1):
                take(1, 0, part)
            products(it, 0)
        for part in (0, 1):
            for d in (-2, 2):
                s = -1 if d > 0 else 1
                pass_on(1, d, part, ("z", s), (1, d - s))
                if (part == 0) == (d > 0):
                    pass_on(1, d, part, ("z", 2 * s), (1, 4))
        if it == 0:
            for part in (0, 1):
                take(1, 0, part)
            products(it, 0)
            build(GROUPS[2])
        for dx, dz in GROUPS[1]:
            for part in (0, 1):
                take(dx, dz, part)
        products(it, 1)
        for dx, dz in GROUPS[2]:
            for part in (0, 1):
                take(dx, dz, part)

        core_copies = {}

        def finish(kk, xx):
            for first in range(xx * PIECES, (xx + 1) * PIECES, ROWS):
                at = kk * 2 * PIECES + first
                part = product(it, 2, at) + acc[at : at + ROWS, :]
                if kk:
                    acc[at : at + ROWS, :] = part
                else:
                    csend[it, first : first + ROWS, :] = part.astype(bf16)
                    where = pl.ds(first, ROWS)
                    core_copies[first // ROWS] = send(
                        csend.at[it, where], crecv.at[it, where], "C"
                    )

        def local(j, xx, top=0, rows=BLK):
            first = xx * PIECES + ORDER.index(j) * BLK + top
            copy = core_copies.pop(first // ROWS, None)
            if copy is not None:
                copy.wait_recv()
            at = 2 * PIECES + first
            return acc[at : at + rows, :] + crecv[it, first : first + rows, :].astype(f32)

        sent = {}

        def ship(n, xx, value, way, rows=BLK):
            ysend[it, xx, n, 0:rows, :] = value.astype(bf16)
            where = pl.ds(0, rows)
            sent[n, xx] = send(ysend.at[it, xx, n, where], yrecv.at[it, xx, n, where], way)

        def landed(n, xx, rows=BLK):
            sent.pop((n, xx)).wait_recv()
            return yrecv[it, xx, n, 0:rows, :].astype(f32)

        def far(xx):
            ship(0, xx, local(4, xx, 0, half), ("y", 2), half)
            ship(1, xx, local(4, xx, half, half), ("y", -2), half)
            ship(2, xx, local(3, xx), ("y", 1))
            ship(3, xx, local(-3, xx), ("y", -1))

        def near(xx):
            ship(4, xx, local(1, xx), ("y", 1))
            ship(5, xx, local(-1, xx), ("y", -1))

        def middle(xx):
            total = local(2, xx) + landed(2, xx)
            ship(
                6, xx,
                jnp.concatenate([total[:half] + landed(0, xx, half), total[half:]], axis=0),
                ("y", 2),
            )
            total = local(-2, xx) + landed(3, xx)
            ship(
                7, xx,
                jnp.concatenate([total[:half], total[half:] + landed(1, xx, half)], axis=0),
                ("y", -2),
            )

        def gathered(xx):
            total = local(0, xx)
            for n in (4, 5, 6, 7):
                total = total + landed(n, xx)
            return total

        finish(0, 0)
        finish(1, 0)
        far(0)
        finish(0, 1)
        finish(1, 1)
        far(1)
        near(0)
        middle(0)
        near(1)
        middle(1)
        xsend[it] = gathered(0).astype(bf16)
        across = send(xsend.at[it], xrecv.at[it], "H")
        mine[...] = gathered(1)
        across.wait_recv()
        total = mine[...] + xrecv[it].astype(f32)
        mixed = jnp.where(covered[...] > 0.5, base[...], factor[...] * total + base[...])
        if it == ITERS - 1:
            out_ref[...] = mixed.astype(bf16)
        else:
            src[it + 1, slot(0, 0) : slot(0, 0) + BLK, :] = mixed.astype(bf16)

    for copy in started:
        copy.wait_send()


COPIES = (30 + 4 + 16 + 1) * ITERS


def local(prior, inv_degree, seed_rows, seed_scores, block_mask, block_row, block_col, block_live):
    slots, width = block_mask.shape[0], prior.shape[1]
    vmem = pl.BlockSpec(memory_space=pltpu.VMEM)
    smem = pl.BlockSpec(memory_space=pltpu.SMEM)
    bf16, f32 = jnp.bfloat16, jnp.float32
    targets, sources = 4 * NY * BLK, 2 * NZ * BLK
    return pl.pallas_call(
        kernel,
        out_shape=jax.ShapeDtypeStruct(prior.shape, bf16),
        in_specs=[vmem, vmem, vmem, vmem, pl.BlockSpec(memory_space=pl.ANY), smem, smem, smem],
        out_specs=vmem,
        scratch_shapes=[
            pltpu.VMEM((slots, BLK, BLK), jnp.int32),
            pltpu.VMEM((slots + 1, BLK, BLK), bf16),
            pltpu.VMEM((targets, sources), bf16),
            pltpu.VMEM((ITERS, sources, width), bf16),
            pltpu.VMEM((ITERS, targets // 2, width), bf16),
            pltpu.VMEM((ITERS, targets // 2, width), bf16),
            pltpu.VMEM((targets, width), f32),
            pltpu.VMEM((ITERS, 2, 8, BLK, width), bf16),
            pltpu.VMEM((ITERS, 2, 8, BLK, width), bf16),
            pltpu.VMEM((ITERS, BLK, width), bf16),
            pltpu.VMEM((ITERS, BLK, width), bf16),
            pltpu.VMEM((BLK, width), f32),
            pltpu.VMEM((BLK, width), f32),
            pltpu.VMEM((BLK, width), f32),
            pltpu.VMEM((BLK, width), f32),
            pltpu.VMEM((8, 128), jnp.int32),
            pltpu.SMEM((8, 128), jnp.int32),
            pltpu.SemaphoreType.DMA((COPIES,)),
            pltpu.SemaphoreType.DMA((COPIES,)),
            pltpu.SemaphoreType.DMA((2,)),
        ],
        compiler_params=pltpu.CompilerParams(
            collective_id=0, has_side_effects=True, vmem_limit_bytes=56 * 1024 * 1024
        ),
        name="propagate",
    )(
        prior,
        inv_degree.reshape(1, -1),
        seed_rows.reshape(1, -1),
        seed_scores,
        block_mask,
        block_row,
        block_col,
        block_live,
    )


def solution(mesh):
    return jax.shard_map(
        local,
        mesh=mesh,
        in_specs=(
            P(("row", "col"), None),
            P(("row", "col")),
            P(("row", "col")),
            P(("row", "col"), None),
            P(("row", "col"), None, None),
            P(("row", "col")),
            P(("row", "col")),
            P(("row", "col")),
        ),
        out_specs=P(("row", "col"), None),
        check_vma=False,
    )
```

time: 509 us -> 88.2 us (0.17)
  waiting for transfers between devices: 394 us -> 0 us
  Pallas kernels: 0 us -> 85.8 us
  other arithmetic: 58.2 us -> 0 us
  matrix products: 19.5 us -> 0 us
  local copies, waits for them, and re-layouts: 18.8 us -> 1.47 us
  between operations: 13.8 us -> 0.66 us
    reduce_scatter x2 -> x0, waiting for transfers between devices: 260 us -> none  [local(): lax.psum_scatter(summed.astype(jnp.bfloat16), 'row', scatter_dimension=0,...]
    all_gather x2 -> x0, waiting for transfers between devices: 134 us -> none  [local(): sources = lax.all_gather(labels, 'col', axis=0, tiled=True)]
    pallas_call x0 -> x1, Pallas kernels: none -> 85.8 us  [local(): pl.pallas_call(kernel, out_shape=jax.ShapeDtypeStruct(prior.shape, bf16),...]
    scatter-add x2 -> x0, other arithmetic: 46.8 us -> none  [local(): jnp.zeros((target_blocks, side, width), jnp.float32).at[block_row]]
    dot_general x3 -> x0, matrix products: 19.5 us -> none  [the longest x2 17.7 us: local(): jnp.einsum('sij,sjl->sil', weights, picked, preferred_element_type=jnp.fl...]
    gather x2 -> x0, local copies, waits for them, and re-layouts: 13.6 us -> none  [local(): picked = jnp.take(src_blocks, block_col, axis=0)]
    convert_element_type x3 -> x0, other arithmetic: 9.24 us -> none  [the longest x2 7.66 us: local(): summed.astype(jnp.bfloat16)]
    another operation x2 -> x0, local copies, waits for them, and re-layouts: 5.12 us -> none
  transfers between devices with their start and end apart: 4 -> 0, of which waited for: 4 -> 0; matrix products, arithmetic and copies ran while one was open for 0% -> 0% of each run, Pallas kernels for 0% -> 0%
where the time goes in v2:
time: 88.2 us; the launch traced here: 88 us
  Pallas kernels  85.8 us (97%)
  local copies, waits for them, and re-layouts  1.47 us (2%)
    pallas_call x1, Pallas kernels, local(): pl.pallas_call(kernel, out_shape=jax.ShapeDtypeStruct(prior.shape, bf16),...  85.8 us

profile of v2, /device:TPU:1, one launch (start us, length us, event | category | flops | bytes accessed | tf_op | source)
XLA Modules:
  0.0 88.0 jit_solution(15780729545036223916)
XLA Ops:
  0.7 85.8 %propagate.1 = bf16[128,256]{1,0:T(8,128)(2,1)} custom-call(bf16[128,256]{1,0:T(8,128)(2,1)} %prior_ref.1, f32[1,128]{1,0:T(1,128)} %bitcast.2, s32[1,16]{1,0:T(1,128)} %bitcast.3, bf16[16,256]{1,0:T(8,128)(2,1)} %seed_scores_ref.1, s32[72,128,128]{2,1,0:T(8,128)} %mask_hbm.1, s32[72]{0:T(128)} %brow_ref.1, s32[72]{0:T(128)} %bcol_ref.1, s32[1]{0:T(128)S(6)} %copy.10.live_ref), custom_call_target="tpu_custom_call" | custom-call | tf_op jit(solution)/shard_map/propagate/pallas_call | solution.py:318
  86.5 1.5 %copy.11 = bf16[128,256]{1,0:T(8,128)(2,1)} copy(bf16[128,256]{1,0:T(8,128)(2,1)} %propagate.1) | data formatting | bytes 131072

commit v3 on v2

--- a/solution.py
+++ b/solution.py
@@ -26,13 +26,13 @@
 
 
 def kernel(
-    prior_ref, inv_ref, seed_rows_ref, seed_scores_ref, mask_hbm, brow_ref, bcol_ref, live_ref,
+    prior_hbm, inv_hbm, seed_rows_hbm, seed_scores_hbm, mask_hbm, brow_hbm, bcol_hbm, live_hbm,
     out_ref,
-    mask_v, wblk, weights, src, csend, crecv, acc, ysend, yrecv, xsend, xrecv, mine,
+    inv_ref, seed_rows_ref, seed_scores_ref, brow_ref, bcol_ref, live_ref, mask_v, wblk, weights, src, csend, crecv, acc, ysend, yrecv,
     base, factor, covered, table_v, table_s, send_sem, recv_sem, local_sem,
 ):
     f32, bf16 = jnp.float32, jnp.bfloat16
-    width = prior_ref.shape[1]
+    width = out_ref.shape[1]
     row, col = lax.axis_index("row"), lax.axis_index("col")
     core = row % 2
     y = (row // 2) % NY
@@ -58,15 +58,30 @@
     for d in (1, 2, -1, -2):
         peers["z", d] = along_z(d)
         peers["y", d] = along_y(d)
-
-    mask_copy = pltpu.make_async_copy(mask_hbm, mask_v, local_sem.at[0])
-    mask_copy.start()
+    for d in (1, -1):
+        peers["h", d] = (rowof(1 - xh, (y + d + NY) % NY, core), col)
 
     barrier = pltpu.get_barrier_semaphore()
     for peer in peers.values():
         pl.semaphore_signal(barrier, inc=1, device_id=peer, device_id_type=pl.DeviceIdType.MESH)
 
-    src[0, slot(0, 0) : slot(0, 0) + BLK, :] = prior_ref[...]
+    own_rows = pl.ds(slot(0, 0), BLK)
+    fetches = [
+        pltpu.make_async_copy(source, target, local_sem.at[2 + n])
+        for n, (source, target) in enumerate((
+            (brow_hbm, brow_ref),
+            (bcol_hbm, bcol_ref),
+            (live_hbm, live_ref),
+            (prior_hbm, src.at[0, own_rows]),
+            (inv_hbm, inv_ref),
+            (seed_rows_hbm, seed_rows_ref),
+            (seed_scores_hbm, seed_scores_ref),
+        ))
+    ]
+    for fetch in fetches:
+        fetch.start()
+    mask_copy = pltpu.make_async_copy(mask_hbm, mask_v, local_sem.at[0])
+    mask_copy.start()
 
     started = []
 
@@ -85,9 +100,17 @@
         return copy
 
     def prepare_table():
-        spot = lax.broadcasted_iota(jnp.int32, (8, 128), 0) * 128 + lax.broadcasted_iota(
-            jnp.int32, (8, 128), 1
-        )
+        q = lax.broadcasted_iota(jnp.int32, (8, 128), 0)
+        lane = lax.broadcasted_iota(jnp.int32, (8, 128), 1)
+        p, place = lane // len(SLOTS), lane % len(SLOTS)
+        j, dx, dz = (jnp.zeros((8, 128), jnp.int32) for _ in range(3))
+        for n, value in enumerate(ORDER):
+            j = jnp.where(p == n, value, j)
+        for n, pos in enumerate(SLOTS):
+            dx = jnp.where(place == n, pos[0], dx)
+            dz = jnp.where(place == n, pos[1], dz)
+        b = rowof((xh + 1 + q % 2) % 2, (y + j + NY) % NY, (core + 1 + q // 2) % 2)
+        spot = jnp.where(q < 4, b * (2 * NZ) + ((xl + dx) % 2) * NZ + (z + dz) % NZ, -2)
         live = live_ref[0]
 
         def mark(s, table):
@@ -111,7 +134,7 @@
         )
         inv = jnp.sum(jnp.where(eye, inv_ref[...], 0.0), axis=1, keepdims=True)
         factor[...] = jnp.broadcast_to(MIX_RATE * inv, (BLK, width))
-        base[...] = jnp.where(cov > 0.5, seeded, (1.0 - MIX_RATE) * prior_ref[...].astype(f32))
+        base[...] = jnp.where(cov > 0.5, seeded, (1.0 - MIX_RATE) * src[0, 0:BLK, :].astype(f32))
 
     def convert():
         mask_copy.wait()
@@ -124,15 +147,11 @@
     def build(group):
         @pl.loop(0, 4)
         def _(q):
-            kk = q // 2
-            xx = q % 2
-            for p, j in enumerate(ORDER):
-                b = rowof((xh + 1 + xx) % 2, (y + j + NY) % NY, (core + 1 + kk) % 2)
+            for p in range(len(ORDER)):
                 first = pl.multiple_of(q * PIECES + p * BLK, BLK)
-                for dx, dz in group:
-                    c = ((xl + dx) % 2) * NZ + (z + dz) % NZ
-                    which = table_s[b // 8, (b % 8) * 16 + c]
-                    weights[pl.ds(first, BLK), slot(dx, dz) : slot(dx, dz) + BLK] = wblk[which]
+                for pos in group:
+                    which = table_s[q, p * len(SLOTS) + SLOTS.index(pos)]
+                    weights[pl.ds(first, BLK), slot(*pos) : slot(*pos) + BLK] = wblk[which]
 
     def product(it, n, first):
         k = slot(*GROUPS[n][0])
@@ -151,8 +170,6 @@
             acc[first : first + ROWS, :] = part
 
     half = BLK // 2
-    table_copy = prepare_table()
-    prepare_labels()
     pl.semaphore_wait(barrier, len(peers))
 
     for it in range(ITERS):
@@ -168,9 +185,10 @@
 
         def pass_on(dx, dz, part, way, there):
             take(dx, dz, part)
-            coming[there[0], there[1] % NZ, part] = send(
-                block((dx, dz), part), block(there, part), way
-            )
+            source = block((dx, dz), part)
+            if it == 0 and (dx, dz) == (0, 0):
+                source = prior_hbm.at[pl.ds(part * half, half)]
+            coming[there[0], there[1] % NZ, part] = send(source, block(there, part), way)
 
         for part in (0, 1):
             pass_on(0, 0, part, ("z", 2), (0, -2))
@@ -180,7 +198,11 @@
             pass_on(0, 0, part, ("z", 1), (0, -1))
             pass_on(0, 0, part, ("z", -1), (0, 1))
         if it == 0:
+            for fetch in fetches:
+                fetch.wait()
+            table_copy = prepare_table()
             convert()
+            table_copy.wait()
         for part in (0, 1):
             for d in (-2, 2):
                 s = -1 if d > 0 else 1
@@ -192,8 +214,8 @@
             for d in (-1, 1):
                 pass_on(0, d, part, "X", (1, d))
         if it == 0:
-            table_copy.wait()
-            build(GROUPS[0] + GROUPS[1])
+            build(GROUPS[0])
+            build(GROUPS[1])
         else:
             for part in (0, 1):
                 take(1, 0, part)
@@ -207,8 +229,8 @@
         if it == 0:
             for part in (0, 1):
                 take(1, 0, part)
+            build(GROUPS[2])
             products(it, 0)
-            build(GROUPS[2])
         for dx, dz in GROUPS[1]:
             for part in (0, 1):
                 take(dx, dz, part)
@@ -257,29 +279,28 @@
             ship(2, xx, local(3, xx), ("y", 1))
             ship(3, xx, local(-3, xx), ("y", -1))
 
-        def near(xx):
-            ship(4, xx, local(1, xx), ("y", 1))
-            ship(5, xx, local(-1, xx), ("y", -1))
+        def across():
+            ship(4, 0, local(1, 0), "H")
+            ship(5, 0, local(-1, 0), "H")
+            ship(8, 0, local(0, 0), "H")
 
         def middle(xx):
             total = local(2, xx) + landed(2, xx)
             ship(
                 6, xx,
                 jnp.concatenate([total[:half] + landed(0, xx, half), total[half:]], axis=0),
-                ("y", 2),
+                ("yh"[xx == 0], 1),
             )
             total = local(-2, xx) + landed(3, xx)
             ship(
                 7, xx,
                 jnp.concatenate([total[:half], total[half:] + landed(1, xx, half)], axis=0),
-                ("y", -2),
+                ("yh"[xx == 0], -1),
             )
 
-        def gathered(xx):
-            total = local(0, xx)
-            for n in (4, 5, 6, 7):
-                total = total + landed(n, xx)
-            return total
+        def near(n, d):
+            total = local(d, 1) + landed(4 + n, 0) + landed(6 + n, 0) + landed(6 + n, 1)
+            ship(4 + n, 1, total, ("y", d))
 
         finish(0, 0)
         finish(1, 0)
@@ -287,15 +308,15 @@
         finish(0, 1)
         finish(1, 1)
         far(1)
-        near(0)
+        across()
+        if it == 0:
+            prepare_labels()
         middle(0)
-        near(1)
         middle(1)
-        xsend[it] = gathered(0).astype(bf16)
-        across = send(xsend.at[it], xrecv.at[it], "H")
-        mine[...] = gathered(1)
-        across.wait_recv()
-        total = mine[...] + xrecv[it].astype(f32)
+        near(0, 1)
+        near(1, -1)
+        total = local(0, 1) + landed(8, 0)
+        total = total + landed(4, 1) + landed(5, 1)
         mixed = jnp.where(covered[...] > 0.5, base[...], factor[...] * total + base[...])
         if it == ITERS - 1:
             out_ref[...] = mixed.astype(bf16)
@@ -306,21 +327,25 @@
         copy.wait_send()
 
 
-COPIES = (30 + 4 + 16 + 1) * ITERS
+COPIES = (30 + 4 + 17) * ITERS
 
 
 def local(prior, inv_degree, seed_rows, seed_scores, block_mask, block_row, block_col, block_live):
     slots, width = block_mask.shape[0], prior.shape[1]
-    vmem = pl.BlockSpec(memory_space=pltpu.VMEM)
-    smem = pl.BlockSpec(memory_space=pltpu.SMEM)
     bf16, f32 = jnp.bfloat16, jnp.float32
     targets, sources = 4 * NY * BLK, 2 * NZ * BLK
     return pl.pallas_call(
         kernel,
         out_shape=jax.ShapeDtypeStruct(prior.shape, bf16),
-        in_specs=[vmem, vmem, vmem, vmem, pl.BlockSpec(memory_space=pl.ANY), smem, smem, smem],
-        out_specs=vmem,
+        in_specs=[pl.BlockSpec(memory_space=pl.ANY)] * 8,
+        out_specs=pl.BlockSpec(memory_space=pltpu.VMEM),
         scratch_shapes=[
+            pltpu.VMEM((1, inv_degree.shape[0]), f32),
+            pltpu.VMEM((1, seed_rows.shape[0]), jnp.int32),
+            pltpu.VMEM(seed_scores.shape, bf16),
+            pltpu.SMEM(block_row.shape, jnp.int32),
+            pltpu.SMEM(block_col.shape, jnp.int32),
+            pltpu.SMEM(block_live.shape, jnp.int32),
             pltpu.VMEM((slots, BLK, BLK), jnp.int32),
             pltpu.VMEM((slots + 1, BLK, BLK), bf16),
             pltpu.VMEM((targets, sources), bf16),
@@ -328,11 +353,8 @@
             pltpu.VMEM((ITERS, targets // 2, width), bf16),
             pltpu.VMEM((ITERS, targets // 2, width), bf16),
             pltpu.VMEM((targets, width), f32),
-            pltpu.VMEM((ITERS, 2, 8, BLK, width), bf16),
-            pltpu.VMEM((ITERS, 2, 8, BLK, width), bf16),
-            pltpu.VMEM((ITERS, BLK, width), bf16),
-            pltpu.VMEM((ITERS, BLK, width), bf16),
-            pltpu.VMEM((BLK, width), f32),
+            pltpu.VMEM((ITERS, 2, 9, BLK, width), bf16),
+            pltpu.VMEM((ITERS, 2, 9, BLK, width), bf16),
             pltpu.VMEM((BLK, width), f32),
             pltpu.VMEM((BLK, width), f32),
             pltpu.VMEM((BLK, width), f32),
@@ -340,7 +362,7 @@
             pltpu.SMEM((8, 128), jnp.int32),
             pltpu.SemaphoreType.DMA((COPIES,)),
             pltpu.SemaphoreType.DMA((COPIES,)),
-            pltpu.SemaphoreType.DMA((2,)),
+            pltpu.SemaphoreType.DMA((9,)),
         ],
         compiler_params=pltpu.CompilerParams(
             collective_id=0, has_side_effects=True, vmem_limit_bytes=56 * 1024 * 1024

time: 88.2 us -> 81.5 us (0.924)
  Pallas kernels: 85.8 us -> 79.2 us
    pallas_call x1, Pallas kernels: 85.8 us -> 79.2 us  [local(): pl.pallas_call(kernel, out_shape=jax.ShapeDtypeStruct(prior.shape, bf16),...]
where the time goes in v3:
time: 81.5 us; the launch traced here: 81.3 us
  Pallas kernels  79.2 us (97%)
  local copies, waits for them, and re-layouts  1.47 us (2%)
    pallas_call x1, Pallas kernels, local(): pl.pallas_call(kernel, out_shape=jax.ShapeDtypeStruct(prior.shape, bf16),...  79.2 us

profile of v3, /device:TPU:1, one launch (start us, length us, event | category | flops | bytes accessed | tf_op | source)
XLA Modules:
  0.0 81.3 jit_solution(17196513423305484828)
XLA Ops:
  0.7 79.2 %propagate.1 = bf16[128,256]{1,0:T(8,128)(2,1)} custom-call(bf16[128,256]{1,0:T(8,128)(2,1)} %prior_hbm.1, f32[1,128]{1,0:T(1,128)} %bitcast.2, s32[1,16]{1,0:T(1,128)} %bitcast.3, bf16[16,256]{1,0:T(8,128)(2,1)} %seed_scores_hbm.1, s32[72,128,128]{2,1,0:T(8,128)} %mask_hbm.1, s32[72]{0:T(128)} %brow_hbm.1, s32[72]{0:T(128)} %bcol_hbm.1, s32[1]{0:T(128)S(6)} %copy.10.live_hbm), custom_call_target="tpu_custom_call" | custom-call | tf_op jit(solution)/shard_map/propagate/pallas_call | solution.py:337
  79.8 1.5 %copy.11 = bf16[128,256]{1,0:T(8,128)(2,1)} copy(bf16[128,256]{1,0:T(8,128)(2,1)} %propagate.1) | data formatting | bytes 131072

commit v4 on v3

--- a/solution.py
+++ b/solution.py
@@ -80,8 +80,14 @@
     ]
     for fetch in fetches:
         fetch.start()
-    mask_copy = pltpu.make_async_copy(mask_hbm, mask_v, local_sem.at[0])
-    mask_copy.start()
+    quarter = slots // 4
+    mask_copies = []
+    for n in range(4):
+        where = pl.ds(n * quarter, quarter if n < 3 else slots - 3 * quarter)
+        mask_copies.append(
+            pltpu.make_async_copy(mask_hbm.at[where], mask_v.at[where], local_sem.at[9 + n])
+        )
+        mask_copies[n].start()
 
     started = []
 
@@ -118,7 +124,9 @@
             key = jnp.where(s < live, key, -1)
             return jnp.where(spot == key, s + 1, table)
 
-        table_v[...] = lax.fori_loop(0, slots, mark, jnp.zeros((8, 128), jnp.int32))
+        table_v[...] = lax.fori_loop(
+            0, slots, mark, jnp.zeros((8, 128), jnp.int32), unroll=8
+        )
         copy = pltpu.make_async_copy(table_v, table_s, local_sem.at[1])
         copy.start()
         return copy
@@ -137,10 +145,11 @@
         base[...] = jnp.where(cov > 0.5, seeded, (1.0 - MIX_RATE) * src[0, 0:BLK, :].astype(f32))
 
     def convert():
-        mask_copy.wait()
+        for copy in mask_copies:
+            copy.wait()
         wblk[0] = jnp.zeros((BLK, BLK), bf16)
 
-        @pl.loop(0, slots)
+        @pl.loop(0, slots, unroll=4)
         def _(s):
             wblk[s + 1] = mask_v[s].astype(f32).astype(bf16)
 
@@ -241,18 +250,16 @@
 
         core_copies = {}
 
-        def finish(kk, xx):
-            for first in range(xx * PIECES, (xx + 1) * PIECES, ROWS):
-                at = kk * 2 * PIECES + first
-                part = product(it, 2, at) + acc[at : at + ROWS, :]
-                if kk:
-                    acc[at : at + ROWS, :] = part
-                else:
-                    csend[it, first : first + ROWS, :] = part.astype(bf16)
-                    where = pl.ds(first, ROWS)
-                    core_copies[first // ROWS] = send(
-                        csend.at[it, where], crecv.at[it, where], "C"
-                    )
+        def finish(kk, xx, n):
+            first = xx * PIECES + n * ROWS
+            at = kk * 2 * PIECES + first
+            part = product(it, 2, at) + acc[at : at + ROWS, :]
+            if kk:
+                acc[at : at + ROWS, :] = part
+            else:
+                csend[it, first : first + ROWS, :] = part.astype(bf16)
+                where = pl.ds(first, ROWS)
+                core_copies[first // ROWS] = send(csend.at[it, where], crecv.at[it, where], "C")
 
         def local(j, xx, top=0, rows=BLK):
             first = xx * PIECES + ORDER.index(j) * BLK + top
@@ -302,12 +309,14 @@
             total = local(d, 1) + landed(4 + n, 0) + landed(6 + n, 0) + landed(6 + n, 1)
             ship(4 + n, 1, total, ("y", d))
 
-        finish(0, 0)
-        finish(1, 0)
+        for kk in (0, 1):
+            for xx in (0, 1):
+                finish(kk, xx, 0)
         far(0)
-        finish(0, 1)
-        finish(1, 1)
         far(1)
+        for kk in (0, 1):
+            for xx in (0, 1):
+                finish(kk, xx, 1)
         across()
         if it == 0:
             prepare_labels()
@@ -362,7 +371,7 @@
             pltpu.SMEM((8, 128), jnp.int32),
             pltpu.SemaphoreType.DMA((COPIES,)),
             pltpu.SemaphoreType.DMA((COPIES,)),
-            pltpu.SemaphoreType.DMA((9,)),
+            pltpu.SemaphoreType.DMA((13,)),
         ],
         compiler_params=pltpu.CompilerParams(
             collective_id=0, has_side_effects=True, vmem_limit_bytes=56 * 1024 * 1024

time: 81.5 us -> 81.2 us (level)
  no operation moved by 1% of the time
where the time goes in v4:
time: 81.2 us; the launch traced here: 81.1 us
  Pallas kernels  78.9 us (97%)
  local copies, waits for them, and re-layouts  1.47 us (2%)
    pallas_call x1, Pallas kernels, local(): pl.pallas_call(kernel, out_shape=jax.ShapeDtypeStruct(prior.shape, bf16),...  78.9 us

profile of v4, /device:TPU:1, one launch (start us, length us, event | category | flops | bytes accessed | tf_op | source)
XLA Modules:
  0.0 81.1 jit_solution(8484664226390819429)
XLA Ops:
  0.7 78.9 %propagate.1 = bf16[128,256]{1,0:T(8,128)(2,1)} custom-call(bf16[128,256]{1,0:T(8,128)(2,1)} %prior_hbm.1, f32[1,128]{1,0:T(1,128)} %bitcast.2, s32[1,16]{1,0:T(1,128)} %bitcast.3, bf16[16,256]{1,0:T(8,128)(2,1)} %seed_scores_hbm.1, s32[72,128,128]{2,1,0:T(8,128)} %mask_hbm.1, s32[72]{0:T(128)} %brow_hbm.1, s32[72]{0:T(128)} %bcol_hbm.1, s32[1]{0:T(128)S(6)} %copy.10.live_hbm), custom_call_target="tpu_custom_call" | custom-call | tf_op jit(solution)/shard_map/propagate/pallas_call | solution.py:346
  79.6 1.5 %copy.11 = bf16[128,256]{1,0:T(8,128)(2,1)} copy(bf16[128,256]{1,0:T(8,128)(2,1)} %propagate.1) | data formatting | bytes 131072

commit v5 on v4

--- a/solution.py
+++ b/solution.py
@@ -225,6 +225,7 @@
         if it == 0:
             build(GROUPS[0])
             build(GROUPS[1])
+            build(GROUPS[2])
         else:
             for part in (0, 1):
                 take(1, 0, part)
@@ -238,7 +239,6 @@
         if it == 0:
             for part in (0, 1):
                 take(1, 0, part)
-            build(GROUPS[2])
             products(it, 0)
         for dx, dz in GROUPS[1]:
             for part in (0, 1):

time: 81.2 us -> 81.3 us (level)
  no operation moved by 1% of the time
where the time goes in v5:
time: 81.3 us; the launch traced here: 81.2 us
  Pallas kernels  79 us (97%)
  local copies, waits for them, and re-layouts  1.47 us (2%)
    pallas_call x1, Pallas kernels, local(): pl.pallas_call(kernel, out_shape=jax.ShapeDtypeStruct(prior.shape, bf16),...  79 us

profile of v5, /device:TPU:1, one launch (start us, length us, event | category | flops | bytes accessed | tf_op | source)
XLA Modules:
  0.0 81.2 jit_solution(5906325761657366691)
XLA Ops:
  0.7 79.0 %propagate.1 = bf16[128,256]{1,0:T(8,128)(2,1)} custom-call(bf16[128,256]{1,0:T(8,128)(2,1)} %prior_hbm.1, f32[1,128]{1,0:T(1,128)} %bitcast.2, s32[1,16]{1,0:T(1,128)} %bitcast.3, bf16[16,256]{1,0:T(8,128)(2,1)} %seed_scores_hbm.1, s32[72,128,128]{2,1,0:T(8,128)} %mask_hbm.1, s32[72]{0:T(128)} %brow_hbm.1, s32[72]{0:T(128)} %bcol_hbm.1, s32[1]{0:T(128)S(6)} %copy.10.live_hbm), custom_call_target="tpu_custom_call" | custom-call | tf_op jit(solution)/shard_map/propagate/pallas_call | solution.py:346
  79.7 1.5 %copy.11 = bf16[128,256]{1,0:T(8,128)(2,1)} copy(bf16[128,256]{1,0:T(8,128)(2,1)} %propagate.1) | data formatting | bytes 131072
